TPU v7x, 32 devices: a whole 2x2x4 slice. The times are simulated.
32 devices in a mesh: freq: 8 (over z, core), tm: 2 (over y), beam: 2 (over x).
Axes of the slice: x: 2, y: 2, z: 4, core: 2. Of those that a mesh axis runs over, the one named last changes fastest.
Arguments:
- raw_samples: bfloat16 [6144, 4096], P(('beam', 'tm'), 'freq'), parts along dimension 0, may hold values from -6 to 6
- filter_taps: bfloat16 [16, 4096], P(None, 'freq'), may hold values from -1.5 to 1.5
- dm_trials: int32 [256], replicated, may hold values from 0 to 1024, as said below
- channel_units: int32 [4096], replicated, may hold values from 0 to 512, as said below
Outputs:
- dm_power: float32 [4, 256, 256], P(('beam', 'tm'), 'freq'), parts along dimension 0
There are 2 independent parts, one for each index of `beam`. A program takes and returns all parts, laid end to end along the dimension named above; an argument that names none is the same for every part. Nothing has to cross between parts.
Inputs may be any that keep to these rules, and one draw needn't show every extreme that they name: Trial d delays a channel of integer delay u by floor(dm_trials[d] * u / 1024) frames. `channel_units`: so that no dispersion delay exceeds 512 frames.
All inputs are finite; a program needn't handle non-finite values.
Results may differ from a plain program's by a relative error of at most 0.0072.
Values may be sent and summed in bfloat16 or wider, within the bound.
A program may use at most 64 MiB of HBM per device.

v0:
```python
import math

import jax
import jax.numpy as jnp
from jax import lax
from jax.sharding import PartitionSpec as P

TAPS = 16
DFT_LEN = 2048
BINS = 256
SHARED = 512
DMS = 256
DM_STEPS = 1024
SEGS_DEV = 1


ramp_block = 32


def passed_along(value, axis, steps):
    count = lax.axis_size(axis)
    leading, last = (max(0, -steps), min(count, count - steps))
    return lax.ppermute(value, axis, [(source, source + steps) for source in range(leading, last)])


def sample_table(members, position, inner_len):
    group_len = inner_len // members
    channels = inner_len * members
    shape = (members, 2, group_len, members, 2, group_len)
    source = lax.broadcasted_iota(jnp.int32, shape, 0)
    parity = lax.broadcasted_iota(jnp.int32, shape, 1)
    offset = lax.broadcasted_iota(jnp.int32, shape, 2)
    target = lax.broadcasted_iota(jnp.int32, shape, 3)
    parity_out = lax.broadcasted_iota(jnp.int32, shape, 4)
    offset_out = lax.broadcasted_iota(jnp.int32, shape, 5)
    first_index = position * group_len + offset
    phases = (inner_len * source * target + first_index * target) % channels
    angles = phases.astype(jnp.float32) * (2.0 * math.pi / channels)
    scale = 1.0 / math.sqrt(members)
    cosine = jnp.cos(angles) * scale
    sine = jnp.sin(angles) * scale
    values = jnp.where(parity == parity_out, cosine, jnp.where(parity == 1, sine, -sine))
    values = values * (offset == offset_out).astype(jnp.float32)
    return values.reshape(2 * inner_len, 2 * inner_len).astype(jnp.bfloat16).astype(jnp.float32)


def channel_table(members, inner_len):
    group_len = inner_len // members
    shape = (members, 2, group_len, 2, inner_len)
    source = lax.broadcasted_iota(jnp.int32, shape, 0)
    parity = lax.broadcasted_iota(jnp.int32, shape, 1)
    offset = lax.broadcasted_iota(jnp.int32, shape, 2)
    parity_out = lax.broadcasted_iota(jnp.int32, shape, 3)
    channel_ids = lax.broadcasted_iota(jnp.int32, shape, 4)
    phases = (source * group_len + offset) * channel_ids % inner_len
    angles = phases.astype(jnp.float32) * (2.0 * math.pi / inner_len)
    scale = 1.0 / math.sqrt(inner_len)
    cosine = jnp.cos(angles) * scale
    sine = jnp.sin(angles) * scale
    values = jnp.where(parity == parity_out, cosine, jnp.where(parity == 1, sine, -sine))
    return values.reshape(2 * inner_len, 2 * inner_len).astype(jnp.bfloat16).astype(jnp.float32)


def time_table():
    shape = (2, BINS, DFT_LEN)
    parity = lax.broadcasted_iota(jnp.int32, shape, 0)
    bin_ids = lax.broadcasted_iota(jnp.int32, shape, 1)
    time_ids = lax.broadcasted_iota(jnp.int32, shape, 2)
    phases = bin_ids * time_ids % DFT_LEN
    angles = phases.astype(jnp.float32) * (2.0 * math.pi / DFT_LEN)
    scale = 1.0 / math.sqrt(DFT_LEN)
    values = jnp.where(parity == 0, jnp.cos(angles) * scale, -jnp.sin(angles) * scale)
    return values.astype(jnp.bfloat16)


def fir_filter(extended, filter_taps):
    taps_wide = filter_taps.astype(jnp.float32)
    wide = extended.astype(jnp.float32)
    out_len = extended.shape[0] - (TAPS - 1)
    total = jnp.zeros((out_len, extended.shape[1]), jnp.float32)
    for tap_id in range(TAPS):
        total = total + taps_wide[tap_id] * wide[TAPS - 1 - tap_id : TAPS - 1 - tap_id + out_len]
    return total.astype(jnp.bfloat16)


def phase_ramp(spectra_part, bin_ids, dm_rows, unit_rows, norm):
    delays = dm_rows[:, None] * unit_rows[None, :] // DM_STEPS
    phases = bin_ids[:, None, None] * delays[None, :, :] % DFT_LEN
    angles = phases.astype(jnp.float32) * (2.0 * math.pi / DFT_LEN)
    cosine = jnp.cos(angles).astype(jnp.bfloat16)
    sine = jnp.sin(angles).astype(jnp.bfloat16)
    cos_part = jnp.einsum("bdc,bxc->bdx", cosine, spectra_part, preferred_element_type=jnp.float32)
    sin_part = jnp.einsum("bdc,bxc->bdx", sine, spectra_part, preferred_element_type=jnp.float32)
    cos_part = cos_part.reshape(cos_part.shape[0], cos_part.shape[1], SEGS_DEV, 2)
    sin_part = sin_part.reshape(sin_part.shape[0], sin_part.shape[1], SEGS_DEV, 2)
    real_part = (cos_part[..., 0] - sin_part[..., 1]) * norm
    imag_part = (sin_part[..., 0] + cos_part[..., 1]) * norm
    return (real_part, imag_part)


def body(raw_samples, filter_taps, dm_trials, channel_units):
    members = lax.axis_size("freq")
    position = lax.axis_index("freq")
    own_len = raw_samples.shape[0]
    inner_len = raw_samples.shape[1]
    group_len = inner_len // members
    channels = inner_len * members
    highest = lax.Precision.HIGHEST
    sample_mix = sample_table(members, position, inner_len)
    channel_mix = channel_table(members, inner_len)
    tail_raw = raw_samples[own_len - (TAPS - 1) :]
    earlier = passed_along(tail_raw, "tm", 1)
    later = passed_along(raw_samples[:SHARED], "tm", -1)
    filtered = fir_filter(jnp.concatenate([earlier, raw_samples, later], 0), filter_taps)
    pieces = jnp.stack([filtered])
    pieces = pieces.reshape(SEGS_DEV, DFT_LEN, members, group_len)
    seg_spec = jnp.einsum(
        "pbu,sugo->sbgpo", time_table(), pieces, preferred_element_type=jnp.float32
    )
    seg_spec = seg_spec.reshape(SEGS_DEV * BINS, 2 * inner_len)
    mixed = jnp.dot(
        lax.all_to_all(seg_spec, "freq", split_axis=1, concat_axis=1, tiled=True),
        sample_mix,
        precision=highest,
    )
    spectra = jnp.dot(
        lax.all_to_all(mixed, "freq", split_axis=1, concat_axis=1, tiled=True),
        channel_mix,
        precision=highest,
    ).astype(jnp.bfloat16)
    spectra = jnp.transpose(spectra.reshape(SEGS_DEV, BINS, 2, inner_len), (1, 0, 2, 3))
    spectra = spectra.reshape(BINS, 2 * SEGS_DEV, inner_len)
    norm = 1.0 / math.sqrt(channels)
    unit_grid = channel_units.reshape(inner_len, members)
    units_local = lax.dynamic_slice_in_dim(unit_grid, position, 1, 1)[:, 0]

    def bin_block(block_id):
        bin_ids = block_id * ramp_block + jnp.arange(ramp_block, dtype=jnp.int32)
        part_spec = lax.dynamic_slice_in_dim(spectra, block_id * ramp_block, ramp_block, 0)
        return phase_ramp(part_spec, bin_ids, dm_trials, units_local, norm)

    real_part, imag_part = lax.map(bin_block, jnp.arange(BINS // ramp_block, dtype=jnp.int32))
    joined = jnp.stack([real_part, imag_part]).reshape(
        2, BINS, DMS // members * lax.axis_size("freq"), SEGS_DEV
    )
    summed = lax.psum_scatter(
        jnp.transpose(joined, (2, 0, 3, 1)), "freq", scatter_dimension=0, tiled=True
    )
    power = summed[:, 0] * summed[:, 0] + summed[:, 1] * summed[:, 1]
    return jnp.transpose(power, (1, 0, 2))


def solution(mesh):
    in_specs = (P(("beam", "tm"), "freq"), P(None, "freq"), P(), P())
    out_specs = P(("beam", "tm"), "freq", None)
    return jax.shard_map(body, mesh=mesh, in_specs=in_specs, out_specs=out_specs, check_vma=False)
```

profile of v0, /device:TPU:0, one launch (start us, length us, event | category | flops | bytes accessed | tf_op | source)
XLA Modules:
  0.0 1238.4 jit_solution(13493817145699765807)
XLA Ops:
  18.2 6.3 collective-permute-done.1
  29.2 21.5 %fusion.43 = bf16[2048,512]{0,1:T(8,128)(2,1)S(1)} fusion(f32[2063,512]{0,1:T(8,128)S(1)} %convert_element_type.78, f32[512]{0:T(512)S(1)} %bitcast.103, f32[512]{0:T(512)S(1)} %bitcast.102, f32[512]{0:T(512)S(1)} %bitcast.101, f32[512]{0:T(512)S(1)} %bitcast.100, f32[512]{0:T(512)S(1)} %bitcast.99, f32[512]{0:T(512)S(1)} %bitcast.98, f32[512]{0:T(512)S(1)} %bitcast.97, ...), kind=kLoop, calls=%fused_computation.74 | loop fusion | flops 33554432 | bytes 69238784 | tf_op jit(solution)/shard_map/convert_element_type | solution.py:83
  50.7 18.8 %fusion.66 = f32[8,64,2,256]{3,1,2,0:T(8,128)} fusion(bf16[2048,8,64,1]{0,2,3,1:T(8,128)(2,1)S(1)} %bitcast.83, pred[2]{0:T(512)(128)(4,1)S(1)} %iota_compare_fusion.1), kind=kOutput, calls=%fused_computation.113 | convolution fusion | flops 1093664768 | bytes 3145730 | tf_op jit(solution)/shard_map/pbu,sugo->sbgpo/dot_general | solution.py:117
  78.3 23.9 %all-to-all-done = f32[256,8,128]{0,2,1:T(8,128)S(1)} async-done(((f32[256,8,128]{0,2,1:T(8,128)}), f32[256,8,128]{0,2,1:T(8,128)S(1)}, u32[]{:S(2)}, u32[]{:S(2)}) %all-to-all-start) | async-done | bytes 1048608 | tf_op jit(solution)/shard_map/all_to_all | solution.py:122
  111.0 25.8 %all-to-all-done.1 = f32[256,8,128]{2,0,1:T(8,128)S(1)} async-done(((f32[256,8,128]{2,0,1:T(8,128)}), f32[256,8,128]{2,0,1:T(8,128)S(1)}, u32[]{:S(2)}, u32[]{:S(2)}) %all-to-all-start.1) | async-done | bytes 1048608 | tf_op jit(solution)/shard_map/all_to_all | solution.py:127
  137.1 19.5 %fusion.100 = bf16[256,1024]{1,0:T(8,128)(2,1)S(1)} fusion(f32[256,1024]{0,1:T(8,128)S(1)} %bitcast.84, s32[1024]{0:T(1024)S(1)} %bitcast.105, s32[1024]{0:T(1024)S(1)} %add.194, s32[1024]{0:T(1024)S(1)} %bitcast.104, s32[1024]{0:T(1024)S(1)} %iota.162, pred[1024]{0:T(1024)(128)(4,1)S(1)} %iota.174), kind=kOutput, calls=%fused_computation.144 | convolution fusion | flops 3243507712 | bytes 1590272 | tf_op jit(solution)/shard_map/dot_general | solution.py:126
  157.1 1017.2 %while.14 = (s32[]{:T(128)}, f32[8,32,256,1]{2,1,0,3:T(8,128)S(1)}, f32[8,32,256,1]{2,1,0,3:T(8,128)S(1)}, s32[8]{0:T(128)S(1)}, s32[256]{0:T(256)S(1)}, /*index...) while((s32[]{:T(128)}, f32[8,32,256,1]{2,1,0,3:T(8,128)S(1)}, ...), condition=%wide.region_1.2_spmd, body=%wide.region_0.1_spmd.sunk | while | flops 161513504 | bytes 2167095 | solution.py:142
  180.6 61.6 %fusion.144 = f32[32,256,1,2]{1,3,0,2:T(2,128)S(1)} fusion(s32[256,512]{1,0:T(8,128)S(1)} %add_select_fusion.6, s32[32]{0:T(128)S(1)} %iota_add_fusion.3, bf16[256,2,512]{2,1,0:T(2,128)(2,1)S(1)} %get-tuple-element.227, s32[]{:T(128)S(6)} %select_n.221), kind=kOutput, calls=%fused_computation.16.clone.3 | convolution fusion | flops 79691776 | bytes 655876 | tf_op jit(solution)/shard_map/while/body/eval_jaxpr/bdc,bxc->bdx/dot_general | solution.py:93
  242.2 61.0 %fusion.143 = f32[32,256,1,2]{1,3,0,2:T(2,128)S(1)} fusion(s32[256,512]{1,0:T(8,128)S(1)} %add_select_fusion.6, s32[32]{0:T(128)S(1)} %iota_add_fusion.3, bf16[256,2,512]{2,1,0:T(2,128)(2,1)S(1)} %get-tuple-element.227, s32[]{:T(128)S(6)} %select_n.221), kind=kOutput, calls=%fused_computation.17.clone.3 | convolution fusion | flops 79691776 | bytes 655876 | tf_op jit(solution)/shard_map/while/body/eval_jaxpr/bdc,bxc->bdx/dot_general | solution.py:92
  305.1 61.6 %fusion.144 = f32[32,256,1,2]{1,3,0,2:T(2,128)S(1)} fusion(s32[256,512]{1,0:T(8,128)S(1)} %add_select_fusion.6, s32[32]{0:T(128)S(1)} %iota_add_fusion.3, bf16[256,2,512]{2,1,0:T(2,128)(2,1)S(1)} %get-tuple-element.227, s32[]{:T(128)S(6)} %select_n.221), kind=kOutput, calls=%fused_computation.16.clone.3 | convolution fusion | flops 79691776 | bytes 655876 | tf_op jit(solution)/shard_map/while/body/eval_jaxpr/bdc,bxc->bdx/dot_general | solution.py:93
  366.6 61.0 %fusion.143 = f32[32,256,1,2]{1,3,0,2:T(2,128)S(1)} fusion(s32[256,512]{1,0:T(8,128)S(1)} %add_select_fusion.6, s32[32]{0:T(128)S(1)} %iota_add_fusion.3, bf16[256,2,512]{2,1,0:T(2,128)(2,1)S(1)} %get-tuple-element.227, s32[]{:T(128)S(6)} %select_n.221), kind=kOutput, calls=%fused_computation.17.clone.3 | convolution fusion | flops 79691776 | bytes 655876 | tf_op jit(solution)/shard_map/while/body/eval_jaxpr/bdc,bxc->bdx/dot_general | solution.py:92
  429.5 61.6 %fusion.144 = f32[32,256,1,2]{1,3,0,2:T(2,128)S(1)} fusion(s32[256,512]{1,0:T(8,128)S(1)} %add_select_fusion.6, s32[32]{0:T(128)S(1)} %iota_add_fusion.3, bf16[256,2,512]{2,1,0:T(2,128)(2,1)S(1)} %get-tuple-element.227, s32[]{:T(128)S(6)} %select_n.221), kind=kOutput, calls=%fused_computation.16.clone.3 | convolution fusion | flops 79691776 | bytes 655876 | tf_op jit(solution)/shard_map/while/body/eval_jaxpr/bdc,bxc->bdx/dot_general | solution.py:93
  491.1 61.0 %fusion.143 = f32[32,256,1,2]{1,3,0,2:T(2,128)S(1)} fusion(s32[256,512]{1,0:T(8,128)S(1)} %add_select_fusion.6, s32[32]{0:T(128)S(1)} %iota_add_fusion.3, bf16[256,2,512]{2,1,0:T(2,128)(2,1)S(1)} %get-tuple-element.227, s32[]{:T(128)S(6)} %select_n.221), kind=kOutput, calls=%fused_computation.17.clone.3 | convolution fusion | flops 79691776 | bytes 655876 | tf_op jit(solution)/shard_map/while/body/eval_jaxpr/bdc,bxc->bdx/dot_general | solution.py:92
  553.9 61.6 %fusion.144 = f32[32,256,1,2]{1,3,0,2:T(2,128)S(1)} fusion(s32[256,512]{1,0:T(8,128)S(1)} %add_select_fusion.6, s32[32]{0:T(128)S(1)} %iota_add_fusion.3, bf16[256,2,512]{2,1,0:T(2,128)(2,1)S(1)} %get-tuple-element.227, s32[]{:T(128)S(6)} %select_n.221), kind=kOutput, calls=%fused_computation.16.clone.3 | convolution fusion | flops 79691776 | bytes 655876 | tf_op jit(solution)/shard_map/while/body/eval_jaxpr/bdc,bxc->bdx/dot_general | solution.py:93
  615.5 61.0 %fusion.143 = f32[32,256,1,2]{1,3,0,2:T(2,128)S(1)} fusion(s32[256,512]{1,0:T(8,128)S(1)} %add_select_fusion.6, s32[32]{0:T(128)S(1)} %iota_add_fusion.3, bf16[256,2,512]{2,1,0:T(2,128)(2,1)S(1)} %get-tuple-element.227, s32[]{:T(128)S(6)} %select_n.221), kind=kOutput, calls=%fused_computation.17.clone.3 | convolution fusion | flops 79691776 | bytes 655876 | tf_op jit(solution)/shard_map/while/body/eval_jaxpr/bdc,bxc->bdx/dot_general | solution.py:92
  678.3 61.6 %fusion.144 = f32[32,256,1,2]{1,3,0,2:T(2,128)S(1)} fusion(s32[256,512]{1,0:T(8,128)S(1)} %add_select_fusion.6, s32[32]{0:T(128)S(1)} %iota_add_fusion.3, bf16[256,2,512]{2,1,0:T(2,128)(2,1)S(1)} %get-tuple-element.227, s32[]{:T(128)S(6)} %select_n.221), kind=kOutput, calls=%fused_computation.16.clone.3 | convolution fusion | flops 79691776 | bytes 655876 | tf_op jit(solution)/shard_map/while/body/eval_jaxpr/bdc,bxc->bdx/dot_general | solution.py:93
  739.9 61.0 %fusion.143 = f32[32,256,1,2]{1,3,0,2:T(2,128)S(1)} fusion(s32[256,512]{1,0:T(8,128)S(1)} %add_select_fusion.6, s32[32]{0:T(128)S(1)} %iota_add_fusion.3, bf16[256,2,512]{2,1,0:T(2,128)(2,1)S(1)} %get-tuple-element.227, s32[]{:T(128)S(6)} %select_n.221), kind=kOutput, calls=%fused_computation.17.clone.3 | convolution fusion | flops 79691776 | bytes 655876 | tf_op jit(solution)/shard_map/while/body/eval_jaxpr/bdc,bxc->bdx/dot_general | solution.py:92
  802.7 61.6 %fusion.144 = f32[32,256,1,2]{1,3,0,2:T(2,128)S(1)} fusion(s32[256,512]{1,0:T(8,128)S(1)} %add_select_fusion.6, s32[32]{0:T(128)S(1)} %iota_add_fusion.3, bf16[256,2,512]{2,1,0:T(2,128)(2,1)S(1)} %get-tuple-element.227, s32[]{:T(128)S(6)} %select_n.221), kind=kOutput, calls=%fused_computation.16.clone.3 | convolution fusion | flops 79691776 | bytes 655876 | tf_op jit(solution)/shard_map/while/body/eval_jaxpr/bdc,bxc->bdx/dot_general | solution.py:93
  864.3 61.0 %fusion.143 = f32[32,256,1,2]{1,3,0,2:T(2,128)S(1)} fusion(s32[256,512]{1,0:T(8,128)S(1)} %add_select_fusion.6, s32[32]{0:T(128)S(1)} %iota_add_fusion.3, bf16[256,2,512]{2,1,0:T(2,128)(2,1)S(1)} %get-tuple-element.227, s32[]{:T(128)S(6)} %select_n.221), kind=kOutput, calls=%fused_computation.17.clone.3 | convolution fusion | flops 79691776 | bytes 655876 | tf_op jit(solution)/shard_map/while/body/eval_jaxpr/bdc,bxc->bdx/dot_general | solution.py:92
  927.1 61.6 %fusion.144 = f32[32,256,1,2]{1,3,0,2:T(2,128)S(1)} fusion(s32[256,512]{1,0:T(8,128)S(1)} %add_select_fusion.6, s32[32]{0:T(128)S(1)} %iota_add_fusion.3, bf16[256,2,512]{2,1,0:T(2,128)(2,1)S(1)} %get-tuple-element.227, s32[]{:T(128)S(6)} %select_n.221), kind=kOutput, calls=%fused_computation.16.clone.3 | convolution fusion | flops 79691776 | bytes 655876 | tf_op jit(solution)/shard_map/while/body/eval_jaxpr/bdc,bxc->bdx/dot_general | solution.py:93
  988.7 61.0 %fusion.143 = f32[32,256,1,2]{1,3,0,2:T(2,128)S(1)} fusion(s32[256,512]{1,0:T(8,128)S(1)} %add_select_fusion.6, s32[32]{0:T(128)S(1)} %iota_add_fusion.3, bf16[256,2,512]{2,1,0:T(2,128)(2,1)S(1)} %get-tuple-element.227, s32[]{:T(128)S(6)} %select_n.221), kind=kOutput, calls=%fused_computation.17.clone.3 | convolution fusion | flops 79691776 | bytes 655876 | tf_op jit(solution)/shard_map/while/body/eval_jaxpr/bdc,bxc->bdx/dot_general | solution.py:92
  1051.5 61.6 %fusion.144 = f32[32,256,1,2]{1,3,0,2:T(2,128)S(1)} fusion(s32[256,512]{1,0:T(8,128)S(1)} %add_select_fusion.6, s32[32]{0:T(128)S(1)} %iota_add_fusion.3, bf16[256,2,512]{2,1,0:T(2,128)(2,1)S(1)} %get-tuple-element.227, s32[]{:T(128)S(6)} %select_n.221), kind=kOutput, calls=%fused_computation.16.clone.3 | convolution fusion | flops 79691776 | bytes 655876 | tf_op jit(solution)/shard_map/while/body/eval_jaxpr/bdc,bxc->bdx/dot_general | solution.py:93
  1113.1 61.0 %fusion.143 = f32[32,256,1,2]{1,3,0,2:T(2,128)S(1)} fusion(s32[256,512]{1,0:T(8,128)S(1)} %add_select_fusion.6, s32[32]{0:T(128)S(1)} %iota_add_fusion.3, bf16[256,2,512]{2,1,0:T(2,128)(2,1)S(1)} %get-tuple-element.227, s32[]{:T(128)S(6)} %select_n.221), kind=kOutput, calls=%fused_computation.17.clone.3 | convolution fusion | flops 79691776 | bytes 655876 | tf_op jit(solution)/shard_map/while/body/eval_jaxpr/bdc,bxc->bdx/dot_general | solution.py:92
  1176.6 53.0 %all-reduce.3.cloned.1.call-done = f32[256,2,1,256]{3,1,2,0:T(2,128)} async-done(((f32[256,2,1,256]{3,1,2,0:T(2,128)}), f32[256,2,1,256]{3,1,2,0:T(2,128)}) %all-reduce.3.cloned.1.call-update) | async-done | bytes 524304
  (101 shorter events, 46.5 us)
Async XLA Ops:
  6.5 8.9 copy-start.1
  8.3 9.9 copy-start
  8.3 16.2 %collective-permute-start.1 = (bf16[512,512]{0,1:T(8,128)(2,1)S(1)}, bf16[512,512]{0,1:T(8,128)(2,1)S(1)}, u32[]{:S(2)}, u32[]{:S(2)}) collective-permute-start(bf16[512,512]{0,1:T(8,128)(2,1)S(1)} %slice.175), channel_id=1, source_target_pairs={{2,0},{3,1},{6,4},{7,5},{10,8},{11,9},{14,12},{15,13},{18,16},{19,... | collective-permute-start | bytes 1572872 | tf_op jit(solution)/shard_map/ppermute | solution.py:23
  10.5 7.7 collective-permute-start
  69.6 32.7 %all-to-all-start = ((f32[256,8,128]{0,2,1:T(8,128)}), f32[256,8,128]{0,2,1:T(8,128)S(1)}, u32[]{:S(2)}, u32[]{:S(2)}) async-start(f32[256,8,128]{0,2,1:T(8,128)} %bitcast.28), calls=%async_computation | async-start | bytes 2097152 | tf_op jit(solution)/shard_map/all_to_all | solution.py:122
  76.4 34.2 %copy-start.3 = (s32[4096]{0:T(1024)S(1)}, s32[4096]{0:T(1024)}, u32[]{:S(2)}) copy-start(s32[4096]{0:T(1024)} %param.9) | copy-start | bytes 49156
  106.7 30.1 %all-to-all-start.1 = ((f32[256,8,128]{2,0,1:T(8,128)}), f32[256,8,128]{2,0,1:T(8,128)S(1)}, u32[]{:S(2)}, u32[]{:S(2)}) async-start(f32[256,8,128]{2,0,1:T(8,128)} %fusion.68), calls=%async_computation.1 | async-start | bytes 2097152 | tf_op jit(solution)/shard_map/all_to_all | solution.py:127
  110.3 1119.3 %all-reduce.3.cloned.1.call-start = ((), (), s32[]{:S(2)}) async-start(), calls=%async_computation.2 | async-start | bytes 1048576
  137.1 19.9 %copy-start.2 = (s32[256]{0:T(256)S(1)}, s32[256]{0:T(256)}, u32[]{:S(2)}) copy-start(s32[256]{0:T(256)} %param.8) | copy-start | bytes 3076
  157.0 1018.3 %copy-start.4 = (u32[32]{0:T(128)S(1)}, u32[32]{0:T(128)}, u32[]{:S(2)}) copy-start(u32[32]{0:T(128)} %constant.158) | copy-start | bytes 388
Sparse Core Ops, SparseCore 0:
  1175.5 54.0 all-reduce.2
where the time goes:
time: 1240 us
  matrix products  1020 us (82%)
  waiting for transfers between devices  112 us (9%)
  other arithmetic  28.6 us (2%)
  loops' own time  27.3 us (2%)
  local copies, waits for them, and re-layouts  16.4 us (1%)
  starting transfers between devices  15.9 us (1%)
  between operations  14.7 us (1%)
    dot_general x8, matrix products, phase_ramp(): jnp.einsum('bdc,bxc->bdx', sine, spectra_part, preferred_element_type=jnp...  493 us
    dot_general x8, matrix products, phase_ramp(): jnp.einsum('bdc,bxc->bdx', cosine, spectra_part, preferred_element_type=j...  488 us
    unnamed x2, waiting for transfers between devices  53 us
    another operation x1, loops' own time, body(): lax.map(bin_block, jnp.arange(BINS // ramp_block, dtype=jnp.int32))  27.3 us
    all_to_all x1, waiting for transfers between devices, body(): lax.all_to_all(mixed, 'freq', split_axis=1, concat_axis=1, tiled=True)  25.8 us
  transfers between devices with their start and end apart: 5, of which 5 were waited for; matrix products, arithmetic and copies ran while one was open for 0% of the time, Pallas kernels for 0%

commit v1 on v0

v1 whole, which is shorter than its diff:
```python
import math

import jax
import jax.numpy as jnp
import numpy as np
from jax import lax
from jax.experimental import pallas as pl
from jax.experimental.pallas import tpu as pltpu
from jax.sharding import PartitionSpec as P

TAPS = 16
DFT_LEN = 2048
BINS = 256
SHARED = 512
DMS = 256
DM_STEPS = 1024
CHANNELS = 4096
RADIX = 8
INNER = CHANNELS // RADIX
CHUNK = 16


def passed_along(value, axis, steps):
    count = lax.axis_size(axis)
    leading, last = (max(0, -steps), min(count, count - steps))
    return lax.ppermute(value, axis, [(source, source + steps) for source in range(leading, last)])


def tables():
    bins = np.arange(BINS)[:, None]
    angle = 2 * np.pi * (bins * np.arange(DFT_LEN)[None, :] % DFT_LEN) / DFT_LEN
    time = np.concatenate([np.cos(angle), -np.sin(angle)], 0) / math.sqrt(DFT_LEN)
    angle = 2 * np.pi * (bins * np.arange(TAPS)[None, :]) / DFT_LEN
    tap = np.concatenate([np.cos(angle), -np.sin(angle)], 0)
    ids = np.arange(INNER)
    angle = 2 * np.pi * (np.arange(RADIX)[:, None] * ids[None, :]) / CHANNELS
    twiddle = np.stack([np.cos(angle), -np.sin(angle)]) / math.sqrt(RADIX)
    angle = 2 * np.pi * (ids[:, None] * ids[None, :] % INNER) / INNER
    cosine, sine = np.cos(angle), np.sin(angle)
    channel = np.block([[cosine, -sine], [sine, cosine]]) / math.sqrt(INNER)
    return (
        jnp.asarray(time, jnp.bfloat16),
        jnp.asarray(tap, jnp.float32),
        jnp.asarray(twiddle, jnp.float32),
        jnp.asarray(channel, jnp.bfloat16),
    )


def unit_circle(phase):
    x = phase.astype(jnp.float32) * (2.0 * math.pi / DFT_LEN)
    y = x * x
    sine, cosine = jnp.full_like(y, -1 / 39916800), jnp.full_like(y, 1 / 479001600)
    for value in (1 / 362880, -1 / 5040, 1 / 120, -1 / 6, 1.0):
        sine = sine * y + value
    for value in (-1 / 3628800, 1 / 40320, -1 / 720, 1 / 24, -0.5, 1.0):
        cosine = cosine * y + value
    return cosine, sine * x


def fill_ramps(ramps, dms, first_bin):
    bins = ramps.shape[0]

    @pl.loop(0, SHARED // CHUNK)
    def _(step):
        row = pl.multiple_of(step * CHUNK, CHUNK)
        units = lax.broadcasted_iota(jnp.int32, (CHUNK, DMS), 0) + (row + 1)
        delays = (units * dms[...]) >> 10
        turn_cos, turn_sin = unit_circle(delays)
        phase = (delays * first_bin) & (DFT_LEN - 1)
        quarter = phase >> 9
        cosine, sine = unit_circle(phase & 511)
        odd = (quarter & 1) == 1
        swapped_cos = jnp.where(odd, -sine, cosine)
        swapped_sin = jnp.where(odd, cosine, sine)
        far = quarter >= 2
        cosine = jnp.where(far, -swapped_cos, swapped_cos)
        sine = jnp.where(far, -swapped_sin, swapped_sin)
        for at in range(bins):
            ramps[at, pl.ds(row, CHUNK), :] = cosine.astype(jnp.bfloat16)
            ramps[at, pl.ds(SHARED + row, CHUNK), :] = sine.astype(jnp.bfloat16)
            if at + 1 < bins:
                cosine, sine = (
                    cosine * turn_cos - sine * turn_sin,
                    sine * turn_cos + cosine * turn_sin,
                )


def dft(real, imag):
    count = len(real)
    if count == 1:
        return real, imag
    er, ei = dft(real[0::2], imag[0::2])
    odr, odi = dft(real[1::2], imag[1::2])
    half = count // 2
    outs = [None] * count
    for k in range(half):
        if k == 0:
            tr, ti = odr[k], odi[k]
        elif 4 * k == count:
            tr, ti = odi[k], -odr[k]
        else:
            c, s = math.cos(2 * math.pi * k / count), math.sin(2 * math.pi * k / count)
            tr, ti = odr[k] * c + odi[k] * s, odi[k] * c - odr[k] * s
        outs[k] = (er[k] + tr, ei[k] + ti)
        outs[k + half] = (er[k] - tr, ei[k] - ti)
    return [o[0] for o in outs], [o[1] for o in outs]


def channelize(held, twiddle, first):
    members, _, bins, width = held.shape
    per = members // RADIX
    for lane in range(INNER // 128):
        src, off = (lane * 128) // width, (lane * 128) % width
        real, imag = [], []
        for n2 in range(RADIX):
            real.append(held[n2 * per + src, 0, :, off : off + 128].astype(jnp.float32))
            imag.append(held[n2 * per + src, 1, :, off : off + 128].astype(jnp.float32))
        real, imag = dft(real, imag)
        cols = slice(lane * 128, lane * 128 + 128)
        cols_imag = slice(INNER + lane * 128, INNER + lane * 128 + 128)
        for k2 in range(RADIX):
            c, s = twiddle[0, k2 : k2 + 1, cols], twiddle[1, k2 : k2 + 1, cols]
            rows = slice(k2 * bins, k2 * bins + bins)
            first[rows, cols] = real[k2] * c - imag[k2] * s
            first[rows, cols_imag] = real[k2] * s + imag[k2] * c


def group_units(spectra, units, bins):
    grouped = jnp.zeros((2 * bins, SHARED), jnp.float32)
    whole = jnp.zeros((2 * bins, INNER), jnp.float32)
    ids = lax.broadcasted_iota(jnp.int32, (SHARED, INNER), 0) + 1
    for k2 in range(RADIX):
        part = spectra[k2 * bins : (k2 + 1) * bins]
        part = jnp.concatenate([part[:, :INNER], part[:, INNER:]], 0)
        part = part.astype(jnp.bfloat16)
        whole += part.astype(jnp.float32)
        same = (ids == units[k2 : k2 + 1, :]).astype(jnp.float32).astype(jnp.bfloat16)
        grouped += lax.dot_general(
            part, same, (((1,), (1,)), ((), ())), preferred_element_type=jnp.float32
        )
    rest = jnp.sum(whole, 1, keepdims=True) - jnp.sum(grouped, 1, keepdims=True)
    return grouped, rest


def tail_kernel(held, units, dms, twiddle, channel, power, ramps, first):
    bins = power.shape[0]
    fill_ramps(ramps, dms, lax.axis_index("freq") * bins)
    channelize(held, twiddle, first)
    spectra = jnp.dot(
        first[...].astype(jnp.bfloat16), channel[...], preferred_element_type=jnp.float32
    )
    grouped, rest = group_units(spectra, units, bins)
    real, imag = grouped[:bins], grouped[bins:]
    upper = jnp.concatenate([real, -imag], 1)
    lower = jnp.concatenate([imag, real], 1)
    for at in range(bins):
        left = jnp.concatenate([upper[at : at + 1], lower[at : at + 1]], 0)
        total = jnp.dot(
            left.astype(jnp.bfloat16), ramps[at], preferred_element_type=jnp.float32
        )
        re = total[0:1] + rest[at : at + 1]
        im = total[1:2] + rest[bins + at : bins + at + 1]
        power[at : at + 1, :] = (re * re + im * im) * (1.0 / CHANNELS)


def body(raw_samples, filter_taps, dm_trials, channel_units):
    members = lax.axis_size("freq")
    own_len, width = raw_samples.shape
    bins = BINS // members
    time, tap, twiddle, channel = tables()
    highest = lax.Precision.HIGHEST
    earlier = passed_along(raw_samples[own_len - (TAPS - 1) :], "tm", 1)
    later = passed_along(raw_samples[:SHARED], "tm", -1)
    spec = jnp.dot(
        time, jnp.concatenate([raw_samples, later], 0), preferred_element_type=jnp.float32
    )
    taps = filter_taps.astype(jnp.float32)
    edge = (earlier.astype(jnp.float32) - later[SHARED - (TAPS - 1) :].astype(jnp.float32))[::-1]
    padded = jnp.concatenate([taps, jnp.zeros_like(taps)], 0)
    fringe = jnp.zeros_like(taps)
    for e in range(1, TAPS):
        fringe = fringe + padded[e : e + TAPS] * edge[e - 1 : e]
    gain = jnp.dot(tap, taps, precision=highest)
    extra = jnp.dot(tap, fringe * (1.0 / math.sqrt(DFT_LEN)), precision=highest)
    sr, si, gr, gi = spec[:BINS], spec[BINS:], gain[:BINS], gain[BINS:]
    seg = jnp.stack([sr * gr - si * gi + extra[:BINS], sr * gi + si * gr + extra[BINS:]])
    seg = seg.astype(jnp.bfloat16).reshape(2, members, bins, width).transpose(1, 0, 2, 3)
    held = lax.all_to_all(seg, "freq", split_axis=0, concat_axis=0, tiled=True)
    units = channel_units.reshape(INNER, RADIX).T
    vmem = pl.BlockSpec(memory_space=pltpu.VMEM)
    power = pl.pallas_call(
        tail_kernel,
        out_shape=jax.ShapeDtypeStruct((bins, DMS), jnp.float32),
        in_specs=[vmem] * 5,
        out_specs=vmem,
        scratch_shapes=[
            pltpu.VMEM((bins, 2 * SHARED, DMS), jnp.bfloat16),
            pltpu.VMEM((RADIX * bins, 2 * INNER), jnp.float32),
        ],
        compiler_params=pltpu.CompilerParams(vmem_limit_bytes=48 * 2**20),
    )(held, units, dm_trials.reshape(1, DMS), twiddle, channel)
    power = lax.all_to_all(power, "freq", split_axis=1, concat_axis=0, tiled=True)
    return power.T[None]


def solution(mesh):
    in_specs = (P(("beam", "tm"), "freq"), P(None, "freq"), P(), P())
    out_specs = P(("beam", "tm"), "freq", None)
    return jax.shard_map(body, mesh=mesh, in_specs=in_specs, out_specs=out_specs, check_vma=False)
```

time: 1240 us -> 62.5 us (0.05)
  matrix products: 1020 us -> 5.4 us
  waiting for transfers between devices: 112 us -> 20.3 us
  loops' own time: 27.3 us -> 0 us
  other arithmetic: 28.6 us -> 1.97 us
  between operations: 14.7 us -> 0.22 us
  local copies, waits for them, and re-layouts: 16.4 us -> 3.77 us
    dot_general x19 -> x4, matrix products: 1020 us -> 5.4 us  [the longest x2 2.87 us: body(): jnp.dot(time, jnp.concatenate([raw_samples, later], 0), preferred_element...]
    unnamed x2 -> x0, waiting for transfers between devices: 53 us -> none
    all_to_all x2 -> x1, waiting for transfers between devices: 49.7 us -> 15.1 us  [body(): held = lax.all_to_all(seg, 'freq', split_axis=0, concat_axis=0, tiled=True)]
    another operation x1 -> x0, loops' own time: 27.3 us -> none  [body(): lax.map(bin_block, jnp.arange(BINS // ramp_block, dtype=jnp.int32))]
    convert_element_type x2 -> x0, other arithmetic: 21.8 us -> none  [the longest x1 21.5 us: fir_filter(): return total.astype(jnp.bfloat16)]
  transfers between devices with their start and end apart: 5 -> 3, of which waited for: 5 -> 2; matrix products, arithmetic and copies ran while one was open for 0% -> 8% of each run, Pallas kernels for 0% -> 0%
where the time goes in v1:
time: 62.5 us; the launch traced here: 62.1 us
  waiting for transfers between devices  20.3 us (32%)
  starting transfers between devices  11.9 us (19%)
  Pallas kernels  10.4 us (17%)
  blocking collectives  8.12 us (13%)
  matrix products  5.4 us (9%)
  local copies, waits for them, and re-layouts  3.77 us (6%)
  other arithmetic  1.97 us (3%)
    all_to_all x1, waiting for transfers between devices, body(): held = lax.all_to_all(seg, 'freq', split_axis=0, concat_axis=0, tiled=True)  15.1 us
    pallas_call x1, Pallas kernels, body(): pl.pallas_call(tail_kernel, out_shape=jax.ShapeDtypeStruct((bins, DMS), j...  10.4 us
    all_to_all x1, blocking collectives, body(): lax.all_to_all(power, 'freq', split_axis=1, concat_axis=0, tiled=True)  8.12 us
    ppermute x2, starting transfers between devices, passed_along(): lax.ppermute(value, axis, [(source, source + steps) for source in range(l...  6.18 us
    all_to_all x1, starting transfers between devices, body(): held = lax.all_to_all(seg, 'freq', split_axis=0, concat_axis=0, tiled=True)  5.71 us
    ppermute x2, waiting for transfers between devices, passed_along(): lax.ppermute(value, axis, [(source, source + steps) for source in range(l...  5.22 us
    dot_general x2, matrix products, body(): jnp.dot(time, jnp.concatenate([raw_samples, later], 0), preferred_element...  2.87 us
    dot_general x1, matrix products, body(): gain = jnp.dot(tap, taps, precision=highest)  1.5 us
  transfers between devices with their start and end apart: 3, of which 2 were waited for; matrix products, arithmetic and copies ran while one was open for 8% of the time, Pallas kernels for 0%

profile of v1, /device:TPU:0, one launch (start us, length us, event | category | flops | bytes accessed | tf_op | source)
XLA Modules:
  0.0 62.1 jit_solution(13070186026020318022)
XLA Ops:
  0.0 1.2 %slice.132 = bf16[512,512]{1,0:T(8,128)(2,1)S(1)} slice(bf16[1536,512]{1,0:T(8,128)(2,1)} %param.8), slice={[0:512], [0:512]} | slice | bytes 1048576 | tf_op jit(solution)/shard_map/slice | solution.py:173
  1.2 1.3 %collective-permute-start = (bf16[512,512]{1,0:T(8,128)(2,1)S(1)}, bf16[512,512]{1,0:T(8,128)(2,1)S(1)}, u32[]{:S(2)}, u32[]{:S(2)}) collective-permute-start(bf16[512,512]{1,0:T(8,128)(2,1)S(1)} %slice.132), channel_id=1, source_target_pairs={{2,0},{3,1},{6,4},{7,5},{10,8},{11,9},{14,12},{15,13},{18,16},{19,... | collective-permute-start | bytes 1572872 | tf_op jit(solution)/shard_map/ppermute | solution.py:26
  2.5 0.7 %slice.138 = bf16[15,512]{1,0:T(8,128)(2,1)S(1)} slice(bf16[1536,512]{1,0:T(8,128)(2,1)} %param.8), slice={[1521:1536], [0:512]} | slice | bytes 30720 | tf_op jit(solution)/shard_map/slice | solution.py:172
  3.2 4.9 %collective-permute-start.1 = (bf16[15,512]{1,0:T(8,128)(2,1)S(1)}, bf16[15,512]{1,0:T(8,128)(2,1)S(1)}, u32[]{:S(2)}, u32[]{:S(2)}) collective-permute-start(bf16[15,512]{1,0:T(8,128)(2,1)S(1)} %slice.138), channel_id=1, source_target_pairs={{0,2},{1,3},{4,6},{5,7},{8,10},{9,11},{12,14},{13,15},{16,18},{17,... | collective-permute-start | bytes 46088 | tf_op jit(solution)/shard_map/ppermute | solution.py:26
  8.1 1.5 %fusion.51 = f32[512,512]{1,0:T(8,128)S(1)} fusion(f32[512,16]{1,0:T(8,128)} %constant.14.clone, bf16[16,512]{1,0:T(8,128)(2,1)} %param.9), kind=kOutput, calls=%fused_computation.59 | convolution fusion | flops 50331648 | bytes 1097728 | tf_op jit(solution)/shard_map/dot_general | solution.py:183
  9.7 0.0 copy-start.3
  9.7 2.4 %fusion.50 = f32[512,512]{1,0:T(8,128)S(1)} fusion(bf16[512,1536]{1,0:T(8,128)(2,1)} %constant.19, bf16[1536,512]{1,0:T(8,128)(2,1)S(1)} %copy-done.5), kind=kOutput, calls=%fused_computation.58 | convolution fusion | flops 805306368 | bytes 4194304 | tf_op jit(solution)/shard_map/dot_general | solution.py:174
  12.2 5.2 %collective-permute-done = bf16[512,512]{1,0:T(8,128)(2,1)S(1)} collective-permute-done((bf16[512,512]{1,0:T(8,128)(2,1)S(1)}, bf16[512,512]{1,0:T(8,128)(2,1)S(1)}, u32[]{:S(2)}, u32[]{:S(2)}) %collective-permute-start) | collective-permute-done | bytes 524320 | tf_op jit(solution)/shard_map/ppermute | solution.py:26
  17.4 1.0 %fusion.4 = f32[512,512]{1,0:T(8,128)S(1)} fusion(f32[512,16]{1,0:T(8,128)S(1)} %copy-done.3, f32[32,512]{1,0:T(8,128)S(1)} %pad_convert_fusion, f32[512]{0:T(512)S(1)} %bitcast.45, f32[512]{0:T(512)S(1)} %bitcast.46, f32[512]{0:T(512)S(1)} %bitcast.47, f32[512]{0:T(512)S(1)} %bitcast.48, f32[512]{0:T(512)S(1)} %bitcast.49, f32[512]{0:T(512)S(1)} %bitcast.50, ...), kind=kOutput, calls=%fused_computation.9 | convolution fusion | flops 50577408 | bytes 1832960 | tf_op jit(solution)/shard_map/dot_general | solution.py:184
  18.5 0.4 convolution_add_fusion
  18.9 0.4 fusion.1
  19.4 0.8 %maximum_bitcast_fusion = bf16[8,2,32,512]{3,2,1,0:T(8,128)(2,1)} fusion(bf16[1,8,32,512]{3,2,0,1:T(8,128)(2,1)S(1)} %bitcast.41, bf16[1,8,32,512]{3,2,0,1:T(8,128)(2,1)S(1)} %bitcast.40), kind=kLoop, calls=%fused_computation.5 | loop fusion | flops 262144 | bytes 1048576 | tf_op jit(solution)/shard_map/transpose | solution.py:187
  20.2 5.7 %all-to-all-start = ((bf16[8,2,32,512]{3,2,1,0:T(8,128)(2,1)}), bf16[8,2,32,512]{3,2,1,0:T(8,128)(2,1)S(1)}, u32[]{:S(2)}, u32[]{:S(2)}) async-start(bf16[8,2,32,512]{3,2,1,0:T(8,128)(2,1)} %maximum_bitcast_fusion), calls=%async_computation | async-start | bytes 1048576 | tf_op jit(solution)/shard_map/all_to_all | solution.py:188
  25.9 0.2 reshape.16
  26.1 0.1 copy.12
  26.2 15.1 %all-to-all-done.held = bf16[8,2,32,512]{3,2,1,0:T(8,128)(2,1)S(1)} async-done(((bf16[8,2,32,512]{3,2,1,0:T(8,128)(2,1)}), bf16[8,2,32,512]{3,2,1,0:T(8,128)(2,1)S(1)}, u32[]{:S(2)}, u32[]{:S(2)}) %all-to-all-start) | async-done | bytes 524320 | tf_op jit(solution)/shard_map/all_to_all | solution.py:188
  41.3 10.4 %shard_map.82 = f32[32,256]{1,0:T(8,128)S(1)} custom-call(bf16[8,2,32,512]{3,2,1,0:T(8,128)(2,1)S(1)} %all-to-all-done.held, s32[8,512]{1,0:T(8,128)S(1)} %bitcast.38, s32[1,256]{1,0:T(1,128)S(1)} %bitcast.39, f32[2,8,512]{2,1,0:T(8,128)S(1)} %copy-done.1, bf16[1024,1024]{1,0:T(8,128)(2,1)S(1)} %copy-done), custom_call_target="tpu_custom_call" | custom-call | tf_op jit(solution)/shard_map/pallas_call | solution.py:191
  51.7 0.1 all_to_all.18
  51.9 0.1 reshape.18
  52.0 8.1 %all_to_all.24 = f32[8,1,1024]{2,1,0:T(1,128)S(1)} all-to-all(f32[8,1,1024]{2,1,0:T(1,128)S(1)} %reshape.18), channel_id=1, replica_groups=mesh['freq'=8,'tm'=2,'beam'=2] {'freq'}, dimensions={0} | all-to-all | bytes 65536 | tf_op jit(solution)/shard_map/all_to_all | solution.py:202
  60.1 0.5 broadcast.2
  60.6 0.7 %reduce = f32[8,1024]{1,0:T(8,128)S(1)} reduce(f32[8,1,1024]{2,1,0:T(1,128)S(1)} %all_to_all.24, f32[]{:T(128)} %broadcast.2), dimensions={1}, to_apply=%all_to_all.19.reduce_sub_computation | reduce | bytes 65540 | tf_op jit(solution)/shard_map/all_to_all | solution.py:202
  61.3 0.1 reshape.19
  61.4 0.7 %copy.14 = f32[256,32]{0,1:T(8,128)} copy(f32[256,32]{1,0:T(8,128)S(1)} %bitcast.42) | data formatting | bytes 65536 | tf_op jit(solution)/shard_map/all_to_all | solution.py:202
  (20 shorter events, 0.1 us)
Async XLA Ops:
  0.0 9.6 %copy-start.5 = (bf16[1536,512]{1,0:T(8,128)(2,1)S(1)}, bf16[1536,512]{1,0:T(8,128)(2,1)}, u32[]{:S(2)}) copy-start(bf16[1536,512]{1,0:T(8,128)(2,1)} %param.8) | copy-start | bytes 4718596
  1.2 16.2 %collective-permute-start = (bf16[512,512]{1,0:T(8,128)(2,1)S(1)}, bf16[512,512]{1,0:T(8,128)(2,1)S(1)}, u32[]{:S(2)}, u32[]{:S(2)}) collective-permute-start(bf16[512,512]{1,0:T(8,128)(2,1)S(1)} %slice.132), channel_id=1, source_target_pairs={{2,0},{3,1},{6,4},{7,5},{10,8},{11,9},{14,12},{15,13},{18,16},{19,... | collective-permute-start | bytes 1572872 | tf_op jit(solution)/shard_map/ppermute | solution.py:26
  3.2 8.9 %collective-permute-start.1 = (bf16[15,512]{1,0:T(8,128)(2,1)S(1)}, bf16[15,512]{1,0:T(8,128)(2,1)S(1)}, u32[]{:S(2)}, u32[]{:S(2)}) collective-permute-start(bf16[15,512]{1,0:T(8,128)(2,1)S(1)} %slice.138), channel_id=1, source_target_pairs={{0,2},{1,3},{4,6},{5,7},{8,10},{9,11},{12,14},{13,15},{16,18},{17,... | collective-permute-start | bytes 46088 | tf_op jit(solution)/shard_map/ppermute | solution.py:26
  9.6 2.5 %copy-start.6 = (bf16[16,512]{1,0:T(8,128)(2,1)S(1)}, bf16[16,512]{1,0:T(8,128)(2,1)}, u32[]{:S(2)}) copy-start(bf16[16,512]{1,0:T(8,128)(2,1)} %param.9) | copy-start | bytes 49156
  9.7 7.8 %copy-start.3 = (f32[512,16]{1,0:T(8,128)S(1)}, f32[512,16]{1,0:T(8,128)}, u32[]{:S(2)}) copy-start(f32[512,16]{1,0:T(8,128)} %constant.14.clone) | copy-start | bytes 98308
  12.1 6.3 %copy-start.4 = (bf16[512,512]{1,0:T(8,128)(2,1)S(1)}, bf16[512,512]{1,0:T(8,128)(2,1)}, u32[]{:S(2)}) copy-start(bf16[512,512]{1,0:T(8,128)(2,1)} %constant.20) | copy-start | bytes 1572868
  18.9 7.0 %copy-start.7 = (s32[4096]{0:T(1024)S(1)}, s32[4096]{0:T(1024)}, u32[]{:S(2)}) copy-start(s32[4096]{0:T(1024)} %param.11) | copy-start | bytes 49156
  19.3 21.9 %copy-start = (bf16[1024,1024]{1,0:T(8,128)(2,1)S(1)}, bf16[1024,1024]{1,0:T(8,128)(2,1)}, u32[]{:S(2)}) copy-start(bf16[1024,1024]{1,0:T(8,128)(2,1)} %constant.16.clone.channel) | copy-start | bytes 6291460
  19.3 21.9 %copy-start.1 = (f32[2,8,512]{2,1,0:T(8,128)S(1)}, f32[2,8,512]{2,1,0:T(8,128)}, u32[]{:S(2)}) copy-start(f32[2,8,512]{2,1,0:T(8,128)} %constant.15.clone.twiddle) | copy-start | bytes 98308
  19.4 21.9 %copy-start.2 = (s32[256]{0:T(256)S(1)}, s32[256]{0:T(256)}, u32[]{:S(2)}) copy-start(s32[256]{0:T(256)} %param.10) | copy-start | bytes 3076
  20.2 21.1 %all-to-all-start = ((bf16[8,2,32,512]{3,2,1,0:T(8,128)(2,1)}), bf16[8,2,32,512]{3,2,1,0:T(8,128)(2,1)S(1)}, u32[]{:S(2)}, u32[]{:S(2)}) async-start(bf16[8,2,32,512]{3,2,1,0:T(8,128)(2,1)} %maximum_bitcast_fusion), calls=%async_computation | async-start | bytes 1048576 | tf_op jit(solution)/shard_map/all_to_all | solution.py:188

commit v2 on v1

--- a/solution.py
+++ b/solution.py
@@ -1,3 +1,4 @@
+import functools
 import math
 
 import jax
@@ -18,12 +19,6 @@
 RADIX = 8
 INNER = CHANNELS // RADIX
 CHUNK = 16
-
-
-def passed_along(value, axis, steps):
-    count = lax.axis_size(axis)
-    leading, last = (max(0, -steps), min(count, count - steps))
-    return lax.ppermute(value, axis, [(source, source + steps) for source in range(leading, last)])
 
 
 def tables():
@@ -125,34 +120,176 @@
             first[rows, cols_imag] = real[k2] * s + imag[k2] * c
 
 
-def group_units(spectra, units, bins):
+def fill_matches(matches, units):
+    ids = lax.broadcasted_iota(jnp.int32, (SHARED, INNER), 0) + 1
+
+    @pl.loop(0, RADIX)
+    def _(k2):
+        same = (ids == units[k2]).astype(jnp.float32)
+        matches[k2] = same.astype(jnp.bfloat16)
+
+
+def group_units(spectra, matches, bins):
     grouped = jnp.zeros((2 * bins, SHARED), jnp.float32)
     whole = jnp.zeros((2 * bins, INNER), jnp.float32)
-    ids = lax.broadcasted_iota(jnp.int32, (SHARED, INNER), 0) + 1
     for k2 in range(RADIX):
         part = spectra[k2 * bins : (k2 + 1) * bins]
         part = jnp.concatenate([part[:, :INNER], part[:, INNER:]], 0)
         part = part.astype(jnp.bfloat16)
         whole += part.astype(jnp.float32)
-        same = (ids == units[k2 : k2 + 1, :]).astype(jnp.float32).astype(jnp.bfloat16)
         grouped += lax.dot_general(
-            part, same, (((1,), (1,)), ((), ())), preferred_element_type=jnp.float32
+            part, matches[k2], (((1,), (1,)), ((), ())), preferred_element_type=jnp.float32
         )
     rest = jnp.sum(whole, 1, keepdims=True) - jnp.sum(grouped, 1, keepdims=True)
     return grouped, rest
 
 
-def tail_kernel(held, units, dms, twiddle, channel, power, ramps, first):
-    bins = power.shape[0]
-    fill_ramps(ramps, dms, lax.axis_index("freq") * bins)
+def partner_order(members):
+    return sorted(range(1, members), key=lambda o: abs(o - members // 2))
+
+
+def kernel(
+    members, segments,
+    raw, time_hbm, channel_hbm, filter_taps, units, dms, tap, twiddle,
+    out,
+    own, time, channel, later, tail, padded, spec, gain, extra, outgoing, held,
+    ramps, matches, first, power_out, power_in,
+    local_sem, halo_send, halo_recv, seg_send, seg_recv, pow_send, pow_recv,
+):
+    me = lax.axis_index("freq")
+    seg = lax.axis_index("tm")
+    own_len, width = own.shape
+    bins = BINS // members
+    kept = DMS // members
+    loads = [
+        pltpu.make_async_copy(raw, own, local_sem.at[0]),
+        pltpu.make_async_copy(time_hbm, time, local_sem.at[1]),
+        pltpu.make_async_copy(channel_hbm, channel, local_sem.at[2]),
+    ]
+    for load in loads:
+        load.start()
+
+    barrier = pltpu.get_barrier_semaphore()
+    order = partner_order(members)
+    for o in order:
+        pl.semaphore_signal(
+            barrier, inc=1, device_id={"freq": lax.rem(me + o, members)},
+            device_id_type=pl.DeviceIdType.MESH,
+        )
+
+    @pl.when(seg > 0)
+    def _():
+        pl.semaphore_signal(
+            barrier, inc=1, device_id={"tm": seg - 1}, device_id_type=pl.DeviceIdType.MESH
+        )
+
+    @pl.when(seg < segments - 1)
+    def _():
+        pl.semaphore_signal(
+            barrier, inc=1, device_id={"tm": seg + 1}, device_id_type=pl.DeviceIdType.MESH
+        )
+
+    pl.semaphore_wait(
+        barrier, members - 1 + jnp.minimum(seg, 1) + jnp.minimum(segments - 1 - seg, 1)
+    )
+
+    def back_copy():
+        return pltpu.make_async_remote_copy(
+            src_ref=raw.at[pl.ds(0, SHARED)], dst_ref=later,
+            send_sem=halo_send.at[0], recv_sem=halo_recv.at[0],
+            device_id={"tm": seg - 1}, device_id_type=pl.DeviceIdType.MESH,
+        )
+
+    def forward_copy():
+        return pltpu.make_async_remote_copy(
+            src_ref=raw.at[pl.ds(own_len - TAPS, TAPS)], dst_ref=tail,
+            send_sem=halo_send.at[1], recv_sem=halo_recv.at[1],
+            device_id={"tm": seg + 1}, device_id_type=pl.DeviceIdType.MESH,
+        )
+
+    @pl.when(seg > 0)
+    def _():
+        back_copy().start()
+
+    @pl.when(seg == 0)
+    def _():
+        tail[...] = jnp.zeros_like(tail)
+
+    @pl.when(seg < segments - 1)
+    def _():
+        forward_copy().start()
+
+    @pl.when(seg == segments - 1)
+    def _():
+        later[...] = jnp.zeros_like(later)
+
+    for load in loads:
+        load.wait()
+    taps = filter_taps[...].astype(jnp.float32)
+    padded[0:TAPS, :] = taps
+    padded[TAPS:, :] = jnp.zeros_like(taps)
+    gain[...] = jnp.dot(
+        tap[...], taps, precision=lax.Precision.HIGHEST, preferred_element_type=jnp.float32
+    )
+    spec[...] = jnp.dot(
+        time[:, 0:own_len], own[...], preferred_element_type=jnp.float32
+    )
+    fill_ramps(ramps, dms, me * bins)
+
+    @pl.when(seg > 0)
+    def _():
+        forward_copy().wait_recv()
+
+    @pl.when(seg < segments - 1)
+    def _():
+        back_copy().wait_recv()
+
+    edge = tail[...].astype(jnp.float32) - later[SHARED - TAPS :, :].astype(jnp.float32)
+    fringe = jnp.zeros_like(taps)
+    for e in range(1, TAPS):
+        fringe = fringe + padded[e : e + TAPS, :] * edge[TAPS - e : TAPS - e + 1]
+    extra[...] = jnp.dot(
+        tap[...], fringe * (1.0 / math.sqrt(DFT_LEN)),
+        precision=lax.Precision.HIGHEST, preferred_element_type=jnp.float32,
+    )
+    spec[...] += jnp.dot(
+        time[:, own_len:], later[...], preferred_element_type=jnp.float32
+    )
+
+    def seg_copy(slot, target):
+        return pltpu.make_async_remote_copy(
+            src_ref=outgoing.at[target], dst_ref=held.at[slot],
+            send_sem=seg_send.at[target], recv_sem=seg_recv.at[slot],
+            device_id={"freq": target}, device_id_type=pl.DeviceIdType.MESH,
+        )
+
+    def block(target):
+        row = pl.multiple_of(target * bins, bins)
+        up, low = pl.ds(row, bins), pl.ds(BINS + row, bins)
+        sr, si, gr, gi = spec[up, :], spec[low, :], gain[up, :], gain[low, :]
+        real = sr * gr - si * gi + extra[up, :]
+        imag = sr * gi + si * gr + extra[low, :]
+        return real.astype(jnp.bfloat16), imag.astype(jnp.bfloat16)
+
+    for o in order:
+        target = lax.rem(me + o, members)
+        outgoing[target, 0], outgoing[target, 1] = block(target)
+        seg_copy(me, target).start()
+    held[me, 0], held[me, 1] = block(me)
+    fill_matches(matches, units)
+
+    for o in order:
+        source = lax.rem(me + o, members)
+        seg_copy(source, source).wait_recv()
     channelize(held, twiddle, first)
     spectra = jnp.dot(
         first[...].astype(jnp.bfloat16), channel[...], preferred_element_type=jnp.float32
     )
-    grouped, rest = group_units(spectra, units, bins)
+    grouped, rest = group_units(spectra, matches, bins)
     real, imag = grouped[:bins], grouped[bins:]
     upper = jnp.concatenate([real, -imag], 1)
     lower = jnp.concatenate([imag, real], 1)
+    rows = []
     for at in range(bins):
         left = jnp.concatenate([upper[at : at + 1], lower[at : at + 1]], 0)
         total = jnp.dot(
@@ -160,47 +297,78 @@
         )
         re = total[0:1] + rest[at : at + 1]
         im = total[1:2] + rest[bins + at : bins + at + 1]
-        power[at : at + 1, :] = (re * re + im * im) * (1.0 / CHANNELS)
+        rows.append((re * re + im * im) * (1.0 / CHANNELS))
+    turned = jnp.concatenate(rows, 0).T
+    for target in range(members):
+        power_out[target] = turned[target * kept : (target + 1) * kept]
+
+    def power_copy(slot, target):
+        return pltpu.make_async_remote_copy(
+            src_ref=power_out.at[target], dst_ref=power_in.at[slot],
+            send_sem=pow_send.at[target], recv_sem=pow_recv.at[slot],
+            device_id={"freq": target}, device_id_type=pl.DeviceIdType.MESH,
+        )
+
+    for o in order:
+        power_copy(me, lax.rem(me + o, members)).start()
+    power_in[me] = power_out[me]
+    for o in order:
+        target = lax.rem(me + o, members)
+        power_copy(target, target).wait_recv()
+    out[...] = jnp.concatenate([power_in[source] for source in range(members)], 1)
+    for o in order:
+        target = lax.rem(me + o, members)
+        seg_copy(target, target).wait_send()
+        power_copy(target, target).wait_send()
+
+    @pl.when(seg > 0)
+    def _():
+        back_copy().wait_send()
+
+    @pl.when(seg < segments - 1)
+    def _():
+        forward_copy().wait_send()
 
 
 def body(raw_samples, filter_taps, dm_trials, channel_units):
     members = lax.axis_size("freq")
     own_len, width = raw_samples.shape
-    bins = BINS // members
+    bins, kept = BINS // members, DMS // members
     time, tap, twiddle, channel = tables()
-    highest = lax.Precision.HIGHEST
-    earlier = passed_along(raw_samples[own_len - (TAPS - 1) :], "tm", 1)
-    later = passed_along(raw_samples[:SHARED], "tm", -1)
-    spec = jnp.dot(
-        time, jnp.concatenate([raw_samples, later], 0), preferred_element_type=jnp.float32
-    )
-    taps = filter_taps.astype(jnp.float32)
-    edge = (earlier.astype(jnp.float32) - later[SHARED - (TAPS - 1) :].astype(jnp.float32))[::-1]
-    padded = jnp.concatenate([taps, jnp.zeros_like(taps)], 0)
-    fringe = jnp.zeros_like(taps)
-    for e in range(1, TAPS):
-        fringe = fringe + padded[e : e + TAPS] * edge[e - 1 : e]
-    gain = jnp.dot(tap, taps, precision=highest)
-    extra = jnp.dot(tap, fringe * (1.0 / math.sqrt(DFT_LEN)), precision=highest)
-    sr, si, gr, gi = spec[:BINS], spec[BINS:], gain[:BINS], gain[BINS:]
-    seg = jnp.stack([sr * gr - si * gi + extra[:BINS], sr * gi + si * gr + extra[BINS:]])
-    seg = seg.astype(jnp.bfloat16).reshape(2, members, bins, width).transpose(1, 0, 2, 3)
-    held = lax.all_to_all(seg, "freq", split_axis=0, concat_axis=0, tiled=True)
-    units = channel_units.reshape(INNER, RADIX).T
+    units = channel_units.reshape(INNER, RADIX).T.reshape(RADIX, 1, INNER)
     vmem = pl.BlockSpec(memory_space=pltpu.VMEM)
+    anywhere = pl.BlockSpec(memory_space=pl.ANY)
+    dma = pltpu.SemaphoreType.DMA
     power = pl.pallas_call(
-        tail_kernel,
-        out_shape=jax.ShapeDtypeStruct((bins, DMS), jnp.float32),
-        in_specs=[vmem] * 5,
+        functools.partial(kernel, members, lax.axis_size("tm")),
+        out_shape=jax.ShapeDtypeStruct((kept, BINS), jnp.float32),
+        in_specs=[anywhere] * 3 + [vmem] * 5,
         out_specs=vmem,
         scratch_shapes=[
+            pltpu.VMEM((own_len, width), jnp.bfloat16),
+            pltpu.VMEM(time.shape, jnp.bfloat16),
+            pltpu.VMEM(channel.shape, jnp.bfloat16),
+            pltpu.VMEM((SHARED, width), jnp.bfloat16),
+            pltpu.VMEM((TAPS, width), jnp.bfloat16),
+            pltpu.VMEM((2 * TAPS, width), jnp.float32),
+            pltpu.VMEM((2 * BINS, width), jnp.float32),
+            pltpu.VMEM((2 * BINS, width), jnp.float32),
+            pltpu.VMEM((2 * BINS, width), jnp.float32),
+            pltpu.VMEM((members, 2, bins, width), jnp.bfloat16),
+            pltpu.VMEM((members, 2, bins, width), jnp.bfloat16),
             pltpu.VMEM((bins, 2 * SHARED, DMS), jnp.bfloat16),
+            pltpu.VMEM((RADIX, SHARED, INNER), jnp.bfloat16),
             pltpu.VMEM((RADIX * bins, 2 * INNER), jnp.float32),
+            pltpu.VMEM((members, kept, bins), jnp.float32),
+            pltpu.VMEM((members, kept, bins), jnp.float32),
+            dma((3,)), dma((2,)), dma((2,)),
+            dma((members,)), dma((members,)), dma((members,)), dma((members,)),
         ],
-        compiler_params=pltpu.CompilerParams(vmem_limit_bytes=48 * 2**20),
-    )(held, units, dm_trials.reshape(1, DMS), twiddle, channel)
-    power = lax.all_to_all(power, "freq", split_axis=1, concat_axis=0, tiled=True)
-    return power.T[None]
+        compiler_params=pltpu.CompilerParams(
+            vmem_limit_bytes=56 * 2**20, collective_id=0, has_side_effects=True
+        ),
+    )(raw_samples, time, channel, filter_taps, units, dm_trials.reshape(1, DMS), tap, twiddle)
+    return power[None]
 
 
 def solution(mesh):

time: 62.5 us -> 45.8 us (0.73)
  Pallas kernels: 10.4 us -> 42.6 us
  waiting for transfers between devices: 20.3 us -> 0 us
  starting transfers between devices: 11.9 us -> 0 us
  blocking collectives: 8.12 us -> 0 us
  matrix products: 5.4 us -> 0 us
  other arithmetic: 1.97 us -> 0 us
  local copies, waits for them, and re-layouts: 3.77 us -> 2.97 us
    pallas_call x1, Pallas kernels: 10.4 us -> 42.6 us  [body(): pl.pallas_call(functools.partial(kernel, members, lax.axis_size('tm')), o...]
    all_to_all x1 -> x0, waiting for transfers between devices: 15.1 us -> none  [body(): held = lax.all_to_all(seg, 'freq', split_axis=0, concat_axis=0, tiled=True)]
    all_to_all x1 -> x0, blocking collectives: 8.12 us -> none  [body(): lax.all_to_all(power, 'freq', split_axis=1, concat_axis=0, tiled=True)]
    ppermute x2 -> x0, starting transfers between devices: 6.18 us -> none  [passed_along(): lax.ppermute(value, axis, [(source, source + steps) for source in range(l...]
    all_to_all x1 -> x0, starting transfers between devices: 5.71 us -> none  [body(): held = lax.all_to_all(seg, 'freq', split_axis=0, concat_axis=0, tiled=True)]
    dot_general x4 -> x0, matrix products: 5.4 us -> none  [the longest x2 2.87 us: body(): jnp.dot(time, jnp.concatenate([raw_samples, later], 0), preferred_element...]
    ppermute x2 -> x0, waiting for transfers between devices: 5.22 us -> none  [passed_along(): lax.ppermute(value, axis, [(source, source + steps) for source in range(l...]
    slice x3 -> x0, local copies, waits for them, and re-layouts: 1.95 us -> none  [the longest x1 1.19 us: body(): later = passed_along(raw_samples[:SHARED], 'tm', -1)]
  transfers between devices with their start and end apart: 3 -> 0, of which waited for: 2 -> 0; matrix products, arithmetic and copies ran while one was open for 8% -> 0% of each run, Pallas kernels for 0% -> 0%
where the time goes in v2:
time: 45.8 us; the launch traced here: 45.5 us
  Pallas kernels  42.6 us (93%)
  local copies, waits for them, and re-layouts  2.97 us (6%)
    pallas_call x1, Pallas kernels, body(): pl.pallas_call(functools.partial(kernel, members, lax.axis_size('tm')), o...  42.6 us
    reshape x3, local copies, waits for them, and re-layouts, body(): units = channel_units.reshape(INNER, RADIX).T.reshape(RADIX, 1, INNER)  1.59 us
    unnamed x1, local copies, waits for them, and re-layouts  1.38 us

profile of v2, /device:TPU:0, one launch (start us, length us, event | category | flops | bytes accessed | tf_op | source)
XLA Modules:
  0.0 45.5 jit_solution(11129752992451785420)
XLA Ops:
  0.0 0.9 %reshape.9 = s32[512,8]{1,0:T(8,128)S(1)} reshape(s32[4096]{0:T(1024)} %param.11) | data formatting | bytes 32768 | tf_op jit(solution)/shard_map/reshape | solution.py:338
  0.9 0.1 copy.9
  1.0 0.6 %reshape.10.units = s32[8,1,512]{2,1,0:T(1,128)} reshape(s32[8,512]{1,0:T(8,128)S(1)} %bitcast.4) | data formatting | bytes 32768 | tf_op jit(solution)/shard_map/reshape | solution.py:338
  1.6 42.6 %shard_map.82 = f32[32,256]{1,0:T(8,128)} custom-call(bf16[1536,512]{1,0:T(8,128)(2,1)} %raw.1, bf16[512,2048]{1,0:T(8,128)(2,1)} %constant.8.clone.time_hbm, bf16[1024,1024]{1,0:T(8,128)(2,1)} %constant.11.clone.channel_hbm, bf16[16,512]{1,0:T(8,128)(2,1)} %filter_taps.1, s32[8,1,512]{2,1,0:T(1,128)} %reshape.10.units, s32[1,256]{1,0:T(1,128)} %bitcast.5, ...), custom_call_target="tpu_custom_call" | custom-call | tf_op jit(solution)/shard_map/pallas_call | solution.py:342
  44.2 1.4 %copy.11 = f32[1,32,256]{2,1,0:T(8,128)} copy(f32[1,32,256]{2,1,0:T(8,128)} %bitcast.3) | data formatting | bytes 65536

commit v3 on v2

--- a/solution.py
+++ b/solution.py
@@ -19,6 +19,7 @@
 RADIX = 8
 INNER = CHANNELS // RADIX
 CHUNK = 16
+LANES = 128
 
 
 def tables():
@@ -52,10 +53,10 @@
     return cosine, sine * x
 
 
-def fill_ramps(ramps, dms, first_bin):
+def fill_ramps(ramps, dms, first_bin, start, stop):
     bins = ramps.shape[0]
 
-    @pl.loop(0, SHARED // CHUNK)
+    @pl.loop(start, stop)
     def _(step):
         row = pl.multiple_of(step * CHUNK, CHUNK)
         units = lax.broadcasted_iota(jnp.int32, (CHUNK, DMS), 0) + (row + 1)
@@ -101,15 +102,15 @@
     return [o[0] for o in outs], [o[1] for o in outs]
 
 
-def channelize(held, twiddle, first):
-    members, _, bins, width = held.shape
+def channelize(held, twiddle, first, slab):
+    slabs, members, _, bins, _ = held.shape
     per = members // RADIX
-    for lane in range(INNER // 128):
-        src, off = (lane * 128) // width, (lane * 128) % width
+    for src in range(per):
+        lane = src * slabs + slab
         real, imag = [], []
         for n2 in range(RADIX):
-            real.append(held[n2 * per + src, 0, :, off : off + 128].astype(jnp.float32))
-            imag.append(held[n2 * per + src, 1, :, off : off + 128].astype(jnp.float32))
+            real.append(held[slab, n2 * per + src, 0].astype(jnp.float32))
+            imag.append(held[slab, n2 * per + src, 1].astype(jnp.float32))
         real, imag = dft(real, imag)
         cols = slice(lane * 128, lane * 128 + 128)
         cols_imag = slice(INNER + lane * 128, INNER + lane * 128 + 128)
@@ -193,23 +194,27 @@
         barrier, members - 1 + jnp.minimum(seg, 1) + jnp.minimum(segments - 1 - seg, 1)
     )
 
-    def back_copy():
+    slabs = width // LANES
+
+    def back_copy(slab):
         return pltpu.make_async_remote_copy(
-            src_ref=raw.at[pl.ds(0, SHARED)], dst_ref=later,
-            send_sem=halo_send.at[0], recv_sem=halo_recv.at[0],
+            src_ref=raw.at[pl.ds(0, SHARED), pl.ds(slab * LANES, LANES)],
+            dst_ref=later.at[slab],
+            send_sem=halo_send.at[1 + slab], recv_sem=halo_recv.at[1 + slab],
             device_id={"tm": seg - 1}, device_id_type=pl.DeviceIdType.MESH,
         )
 
     def forward_copy():
         return pltpu.make_async_remote_copy(
             src_ref=raw.at[pl.ds(own_len - TAPS, TAPS)], dst_ref=tail,
-            send_sem=halo_send.at[1], recv_sem=halo_recv.at[1],
+            send_sem=halo_send.at[0], recv_sem=halo_recv.at[0],
             device_id={"tm": seg + 1}, device_id_type=pl.DeviceIdType.MESH,
         )
 
     @pl.when(seg > 0)
     def _():
-        back_copy().start()
+        for slab in range(slabs):
+            back_copy(slab).start()
 
     @pl.when(seg == 0)
     def _():
@@ -234,54 +239,59 @@
     spec[...] = jnp.dot(
         time[:, 0:own_len], own[...], preferred_element_type=jnp.float32
     )
-    fill_ramps(ramps, dms, me * bins)
 
     @pl.when(seg > 0)
     def _():
         forward_copy().wait_recv()
 
-    @pl.when(seg < segments - 1)
-    def _():
-        back_copy().wait_recv()
-
-    edge = tail[...].astype(jnp.float32) - later[SHARED - TAPS :, :].astype(jnp.float32)
-    fringe = jnp.zeros_like(taps)
-    for e in range(1, TAPS):
-        fringe = fringe + padded[e : e + TAPS, :] * edge[TAPS - e : TAPS - e + 1]
-    extra[...] = jnp.dot(
-        tap[...], fringe * (1.0 / math.sqrt(DFT_LEN)),
-        precision=lax.Precision.HIGHEST, preferred_element_type=jnp.float32,
-    )
-    spec[...] += jnp.dot(
-        time[:, own_len:], later[...], preferred_element_type=jnp.float32
-    )
-
-    def seg_copy(slot, target):
+    def seg_copy(slab, slot, target):
         return pltpu.make_async_remote_copy(
-            src_ref=outgoing.at[target], dst_ref=held.at[slot],
-            send_sem=seg_send.at[target], recv_sem=seg_recv.at[slot],
+            src_ref=outgoing.at[slab, target], dst_ref=held.at[slab, slot],
+            send_sem=seg_send.at[slab, target], recv_sem=seg_recv.at[slab, slot],
             device_id={"freq": target}, device_id_type=pl.DeviceIdType.MESH,
         )
 
-    def block(target):
+    def block(target, cols):
         row = pl.multiple_of(target * bins, bins)
         up, low = pl.ds(row, bins), pl.ds(BINS + row, bins)
-        sr, si, gr, gi = spec[up, :], spec[low, :], gain[up, :], gain[low, :]
+        sr, si, gr, gi = spec[up, cols], spec[low, cols], gain[up, cols], gain[low, cols]
         real = sr * gr - si * gi + extra[up, :]
         imag = sr * gi + si * gr + extra[low, :]
         return real.astype(jnp.bfloat16), imag.astype(jnp.bfloat16)
 
-    for o in order:
-        target = lax.rem(me + o, members)
-        outgoing[target, 0], outgoing[target, 1] = block(target)
-        seg_copy(me, target).start()
-    held[me, 0], held[me, 1] = block(me)
+    steps = SHARED // CHUNK // slabs
+    for slab in range(slabs):
+        cols = slice(slab * LANES, (slab + 1) * LANES)
+
+        @pl.when(seg < segments - 1)
+        def _():
+            back_copy(slab).wait_recv()
+
+        edge = tail[:, cols].astype(jnp.float32)
+        edge = edge - later[slab, SHARED - TAPS :, :].astype(jnp.float32)
+        fringe = jnp.zeros_like(edge)
+        for e in range(1, TAPS):
+            fringe = fringe + padded[e : e + TAPS, cols] * edge[TAPS - e : TAPS - e + 1]
+        extra[...] = jnp.dot(
+            tap[...], fringe * (1.0 / math.sqrt(DFT_LEN)),
+            precision=lax.Precision.HIGHEST, preferred_element_type=jnp.float32,
+        )
+        spec[:, cols] += jnp.dot(
+            time[:, own_len:], later[slab], preferred_element_type=jnp.float32
+        )
+        for o in order:
+            target = lax.rem(me + o, members)
+            outgoing[slab, target, 0], outgoing[slab, target, 1] = block(target, cols)
+            seg_copy(slab, me, target).start()
+        held[slab, me, 0], held[slab, me, 1] = block(me, cols)
+        fill_ramps(ramps, dms, me * bins, slab * steps, (slab + 1) * steps)
     fill_matches(matches, units)
 
-    for o in order:
-        source = lax.rem(me + o, members)
-        seg_copy(source, source).wait_recv()
-    channelize(held, twiddle, first)
+    for slab in range(slabs):
+        for o in order:
+            source = lax.rem(me + o, members)
+            seg_copy(slab, source, source).wait_recv()
+        channelize(held, twiddle, first, slab)
     spectra = jnp.dot(
         first[...].astype(jnp.bfloat16), channel[...], preferred_element_type=jnp.float32
     )
@@ -318,12 +328,14 @@
     out[...] = jnp.concatenate([power_in[source] for source in range(members)], 1)
     for o in order:
         target = lax.rem(me + o, members)
-        seg_copy(target, target).wait_send()
+        for slab in range(slabs):
+            seg_copy(slab, target, target).wait_send()
         power_copy(target, target).wait_send()
 
     @pl.when(seg > 0)
     def _():
-        back_copy().wait_send()
+        for slab in range(slabs):
+            back_copy(slab).wait_send()
 
     @pl.when(seg < segments - 1)
     def _():
@@ -333,7 +345,7 @@
 def body(raw_samples, filter_taps, dm_trials, channel_units):
     members = lax.axis_size("freq")
     own_len, width = raw_samples.shape
-    bins, kept = BINS // members, DMS // members
+    bins, kept, slabs = BINS // members, DMS // members, width // LANES
     time, tap, twiddle, channel = tables()
     units = channel_units.reshape(INNER, RADIX).T.reshape(RADIX, 1, INNER)
     vmem = pl.BlockSpec(memory_space=pltpu.VMEM)
@@ -348,21 +360,21 @@
             pltpu.VMEM((own_len, width), jnp.bfloat16),
             pltpu.VMEM(time.shape, jnp.bfloat16),
             pltpu.VMEM(channel.shape, jnp.bfloat16),
-            pltpu.VMEM((SHARED, width), jnp.bfloat16),
+            pltpu.VMEM((width // LANES, SHARED, LANES), jnp.bfloat16),
             pltpu.VMEM((TAPS, width), jnp.bfloat16),
             pltpu.VMEM((2 * TAPS, width), jnp.float32),
             pltpu.VMEM((2 * BINS, width), jnp.float32),
             pltpu.VMEM((2 * BINS, width), jnp.float32),
-            pltpu.VMEM((2 * BINS, width), jnp.float32),
-            pltpu.VMEM((members, 2, bins, width), jnp.bfloat16),
-            pltpu.VMEM((members, 2, bins, width), jnp.bfloat16),
+            pltpu.VMEM((2 * BINS, LANES), jnp.float32),
+            pltpu.VMEM((slabs, members, 2, bins, LANES), jnp.bfloat16),
+            pltpu.VMEM((slabs, members, 2, bins, LANES), jnp.bfloat16),
             pltpu.VMEM((bins, 2 * SHARED, DMS), jnp.bfloat16),
             pltpu.VMEM((RADIX, SHARED, INNER), jnp.bfloat16),
             pltpu.VMEM((RADIX * bins, 2 * INNER), jnp.float32),
             pltpu.VMEM((members, kept, bins), jnp.float32),
             pltpu.VMEM((members, kept, bins), jnp.float32),
-            dma((3,)), dma((2,)), dma((2,)),
-            dma((members,)), dma((members,)), dma((members,)), dma((members,)),
+            dma((3,)), dma((1 + slabs,)), dma((1 + slabs,)),
+            dma((slabs, members)), dma((slabs, members)), dma((members,)), dma((members,)),
         ],
         compiler_params=pltpu.CompilerParams(
             vmem_limit_bytes=56 * 2**20, collective_id=0, has_side_effects=True

time: 45.8 us -> 38.7 us (0.84)
  Pallas kernels: 42.6 us -> 35.5 us
    pallas_call x1, Pallas kernels: 42.6 us -> 35.5 us  [body(): pl.pallas_call(functools.partial(kernel, members, lax.axis_size('tm')), o...]
where the time goes in v3:
time: 38.7 us; the launch traced here: 38.5 us
  Pallas kernels  35.5 us (92%)
  local copies, waits for them, and re-layouts  2.97 us (8%)
    pallas_call x1, Pallas kernels, body(): pl.pallas_call(functools.partial(kernel, members, lax.axis_size('tm')), o...  35.5 us
    reshape x3, local copies, waits for them, and re-layouts, body(): units = channel_units.reshape(INNER, RADIX).T.reshape(RADIX, 1, INNER)  1.59 us
    unnamed x1, local copies, waits for them, and re-layouts  1.38 us

profile of v3, /device:TPU:0, one launch (start us, length us, event | category | flops | bytes accessed | tf_op | source)
XLA Modules:
  0.0 38.5 jit_solution(10498348542304132239)
XLA Ops:
  0.0 0.9 %reshape.9 = s32[512,8]{1,0:T(8,128)S(1)} reshape(s32[4096]{0:T(1024)} %param.11) | data formatting | bytes 32768 | tf_op jit(solution)/shard_map/reshape | solution.py:350
  0.9 0.1 copy.9
  1.0 0.6 %reshape.10.units = s32[8,1,512]{2,1,0:T(1,128)} reshape(s32[8,512]{1,0:T(8,128)S(1)} %bitcast.4) | data formatting | bytes 32768 | tf_op jit(solution)/shard_map/reshape | solution.py:350
  1.6 35.5 %shard_map.82 = f32[32,256]{1,0:T(8,128)} custom-call(bf16[1536,512]{1,0:T(8,128)(2,1)} %raw.1, bf16[512,2048]{1,0:T(8,128)(2,1)} %constant.8.clone.time_hbm, bf16[1024,1024]{1,0:T(8,128)(2,1)} %constant.11.clone.channel_hbm, bf16[16,512]{1,0:T(8,128)(2,1)} %filter_taps.1, s32[8,1,512]{2,1,0:T(1,128)} %reshape.10.units, s32[1,256]{1,0:T(1,128)} %bitcast.5, ...), custom_call_target="tpu_custom_call" | custom-call | tf_op jit(solution)/shard_map/pallas_call | solution.py:354
  37.1 1.4 %copy.11 = f32[1,32,256]{2,1,0:T(8,128)} copy(f32[1,32,256]{2,1,0:T(8,128)} %bitcast.3) | data formatting | bytes 65536

commit v4 on v3

--- a/solution.py
+++ b/solution.py
@@ -31,7 +31,8 @@
     ids = np.arange(INNER)
     angle = 2 * np.pi * (np.arange(RADIX)[:, None] * ids[None, :]) / CHANNELS
     twiddle = np.stack([np.cos(angle), -np.sin(angle)]) / math.sqrt(RADIX)
-    angle = 2 * np.pi * (ids[:, None] * ids[None, :] % INNER) / INNER
+    spread = ids.reshape(CHANNELS // LANES, LANES // RADIX).T.reshape(-1)
+    angle = 2 * np.pi * (ids[:, None] * spread[None, :] % INNER) / INNER
     cosine, sine = np.cos(angle), np.sin(angle)
     channel = np.block([[cosine, -sine], [sine, cosine]]) / math.sqrt(INNER)
     return (
@@ -122,12 +123,13 @@
 
 
 def fill_matches(matches, units):
-    ids = lax.broadcasted_iota(jnp.int32, (SHARED, INNER), 0) + 1
-
-    @pl.loop(0, RADIX)
-    def _(k2):
-        same = (ids == units[k2]).astype(jnp.float32)
-        matches[k2] = same.astype(jnp.bfloat16)
+    rows, lanes = units.shape
+    ids = lax.broadcasted_iota(jnp.int32, (rows, SHARED), 1) + 1
+    for k2 in range(RADIX):
+        for at in range(lanes // RADIX):
+            lane = at * RADIX + k2
+            same = (units[:, lane : lane + 1] == ids).astype(jnp.float32)
+            matches[k2, at * rows : (at + 1) * rows, :] = same.astype(jnp.bfloat16)
 
 
 def group_units(spectra, matches, bins):
@@ -138,9 +140,7 @@
         part = jnp.concatenate([part[:, :INNER], part[:, INNER:]], 0)
         part = part.astype(jnp.bfloat16)
         whole += part.astype(jnp.float32)
-        grouped += lax.dot_general(
-            part, matches[k2], (((1,), (1,)), ((), ())), preferred_element_type=jnp.float32
-        )
+        grouped += jnp.dot(part, matches[k2], preferred_element_type=jnp.float32)
     rest = jnp.sum(whole, 1, keepdims=True) - jnp.sum(grouped, 1, keepdims=True)
     return grouped, rest
 
@@ -167,7 +167,7 @@
         pltpu.make_async_copy(time_hbm, time, local_sem.at[1]),
         pltpu.make_async_copy(channel_hbm, channel, local_sem.at[2]),
     ]
-    for load in loads:
+    for load in loads[:2]:
         load.start()
 
     barrier = pltpu.get_barrier_semaphore()
@@ -228,14 +228,15 @@
     def _():
         later[...] = jnp.zeros_like(later)
 
-    for load in loads:
-        load.wait()
+    loads[2].start()
     taps = filter_taps[...].astype(jnp.float32)
     padded[0:TAPS, :] = taps
     padded[TAPS:, :] = jnp.zeros_like(taps)
     gain[...] = jnp.dot(
         tap[...], taps, precision=lax.Precision.HIGHEST, preferred_element_type=jnp.float32
     )
+    for load in loads[:2]:
+        load.wait()
     spec[...] = jnp.dot(
         time[:, 0:own_len], own[...], preferred_element_type=jnp.float32
     )
@@ -292,6 +293,7 @@
             source = lax.rem(me + o, members)
             seg_copy(slab, source, source).wait_recv()
         channelize(held, twiddle, first, slab)
+    loads[2].wait()
     spectra = jnp.dot(
         first[...].astype(jnp.bfloat16), channel[...], preferred_element_type=jnp.float32
     )
@@ -347,7 +349,7 @@
     own_len, width = raw_samples.shape
     bins, kept, slabs = BINS // members, DMS // members, width // LANES
     time, tap, twiddle, channel = tables()
-    units = channel_units.reshape(INNER, RADIX).T.reshape(RADIX, 1, INNER)
+    units = channel_units.reshape(CHANNELS // LANES, LANES)
     vmem = pl.BlockSpec(memory_space=pltpu.VMEM)
     anywhere = pl.BlockSpec(memory_space=pl.ANY)
     dma = pltpu.SemaphoreType.DMA
@@ -369,7 +371,7 @@
             pltpu.VMEM((slabs, members, 2, bins, LANES), jnp.bfloat16),
             pltpu.VMEM((slabs, members, 2, bins, LANES), jnp.bfloat16),
             pltpu.VMEM((bins, 2 * SHARED, DMS), jnp.bfloat16),
-            pltpu.VMEM((RADIX, SHARED, INNER), jnp.bfloat16),
+            pltpu.VMEM((RADIX, INNER, SHARED), jnp.bfloat16),
             pltpu.VMEM((RADIX * bins, 2 * INNER), jnp.float32),
             pltpu.VMEM((members, kept, bins), jnp.float32),
             pltpu.VMEM((members, kept, bins), jnp.float32),

time: 38.7 us -> 36.7 us (0.948)
  local copies, waits for them, and re-layouts: 2.97 us -> 1.38 us
  Pallas kernels: 35.5 us -> 35.1 us
    reshape x3 -> x0, local copies, waits for them, and re-layouts: 1.59 us -> none  [body(): units = channel_units.reshape(INNER, RADIX).T.reshape(RADIX, 1, INNER)]
    pallas_call x1, Pallas kernels: 35.5 us -> 35.1 us  [body(): pl.pallas_call(functools.partial(kernel, members, lax.axis_size('tm')), o...]
where the time goes in v4:
time: 36.7 us; the launch traced here: 36.5 us
  Pallas kernels  35.1 us (96%)
  local copies, waits for them, and re-layouts  1.38 us (4%)
    pallas_call x1, Pallas kernels, body(): pl.pallas_call(functools.partial(kernel, members, lax.axis_size('tm')), o...  35.1 us
    unnamed x1, local copies, waits for them, and re-layouts  1.38 us

profile of v4, /device:TPU:0, one launch (start us, length us, event | category | flops | bytes accessed | tf_op | source)
XLA Modules:
  0.0 36.5 jit_solution(7043919772077935186)
XLA Ops:
  0.0 35.1 %shard_map.82 = f32[32,256]{1,0:T(8,128)} custom-call(bf16[1536,512]{1,0:T(8,128)(2,1)} %raw.1, bf16[512,2048]{1,0:T(8,128)(2,1)} %constant.8.clone.time_hbm, bf16[1024,1024]{1,0:T(8,128)(2,1)} %constant.11.clone.channel_hbm, bf16[16,512]{1,0:T(8,128)(2,1)} %filter_taps.1, s32[32,128]{1,0:T(8,128)} %bitcast.4, s32[1,256]{1,0:T(1,128)} %bitcast.5, ...), custom_call_target="tpu_custom_call" | custom-call | tf_op jit(solution)/shard_map/pallas_call | solution.py:356
  35.1 1.4 %copy.10 = f32[1,32,256]{2,1,0:T(8,128)} copy(f32[1,32,256]{2,1,0:T(8,128)} %bitcast.3) | data formatting | bytes 65536

commit v5 on v4

--- a/solution.py
+++ b/solution.py
@@ -260,7 +260,9 @@
         imag = sr * gi + si * gr + extra[low, :]
         return real.astype(jnp.bfloat16), imag.astype(jnp.bfloat16)
 
-    steps = SHARED // CHUNK // slabs
+    early = SHARED // CHUNK // 2
+    steps = early // slabs
+    fill_ramps(ramps, dms, me * bins, 0, early)
     for slab in range(slabs):
         cols = slice(slab * LANES, (slab + 1) * LANES)
 
@@ -285,7 +287,9 @@
             outgoing[slab, target, 0], outgoing[slab, target, 1] = block(target, cols)
             seg_copy(slab, me, target).start()
         held[slab, me, 0], held[slab, me, 1] = block(me, cols)
-        fill_ramps(ramps, dms, me * bins, slab * steps, (slab + 1) * steps)
+        fill_ramps(
+            ramps, dms, me * bins, early + slab * steps, early + (slab + 1) * steps
+        )
     fill_matches(matches, units)
 
     for slab in range(slabs):

time: 36.7 us -> 36.7 us (level)
  no operation moved by 1% of the time
where the time goes in v5:
time: 36.7 us; the launch traced here: 36.5 us
  Pallas kernels  35.1 us (96%)
  local copies, waits for them, and re-layouts  1.38 us (4%)
    pallas_call x1, Pallas kernels, body(): pl.pallas_call(functools.partial(kernel, members, lax.axis_size('tm')), o...  35.1 us
    unnamed x1, local copies, waits for them, and re-layouts  1.38 us

profile of v5, /device:TPU:0, one launch (start us, length us, event | category | flops | bytes accessed | tf_op | source)
XLA Modules:
  0.0 36.5 jit_solution(18157641724290011885)
XLA Ops:
  0.0 35.1 %shard_map.82 = f32[32,256]{1,0:T(8,128)} custom-call(bf16[1536,512]{1,0:T(8,128)(2,1)} %raw.1, bf16[512,2048]{1,0:T(8,128)(2,1)} %constant.8.clone.time_hbm, bf16[1024,1024]{1,0:T(8,128)(2,1)} %constant.11.clone.channel_hbm, bf16[16,512]{1,0:T(8,128)(2,1)} %filter_taps.1, s32[32,128]{1,0:T(8,128)} %bitcast.4, s32[1,256]{1,0:T(1,128)} %bitcast.5, ...), custom_call_target="tpu_custom_call" | custom-call | tf_op jit(solution)/shard_map/pallas_call | solution.py:360
  35.1 1.4 %copy.10 = f32[1,32,256]{2,1,0:T(8,128)} copy(f32[1,32,256]{2,1,0:T(8,128)} %bitcast.3) | data formatting | bytes 65536

commit v6 on v4

--- a/solution.py
+++ b/solution.py
@@ -146,7 +146,7 @@
 
 
 def partner_order(members):
-    return sorted(range(1, members), key=lambda o: abs(o - members // 2))
+    return sorted(range(1, members), key=lambda o: -abs(o - members // 2))
 
 
 def kernel(

time: 36.7 us -> 36.3 us (0.989)
  Pallas kernels: 35.1 us -> 34.7 us
    pallas_call x1, Pallas kernels: 35.1 us -> 34.7 us  [body(): pl.pallas_call(functools.partial(kernel, members, lax.axis_size('tm')), o...]
where the time goes in v6:
time: 36.3 us; the launch traced here: 36.1 us
  Pallas kernels  34.7 us (96%)
  local copies, waits for them, and re-layouts  1.38 us (4%)
    pallas_call x1, Pallas kernels, body(): pl.pallas_call(functools.partial(kernel, members, lax.axis_size('tm')), o...  34.7 us
    unnamed x1, local copies, waits for them, and re-layouts  1.38 us

profile of v6, /device:TPU:0, one launch (start us, length us, event | category | flops | bytes accessed | tf_op | source)
XLA Modules:
  0.0 36.1 jit_solution(15442145149471137446)
XLA Ops:
  0.0 34.7 %shard_map.82 = f32[32,256]{1,0:T(8,128)} custom-call(bf16[1536,512]{1,0:T(8,128)(2,1)} %raw.1, bf16[512,2048]{1,0:T(8,128)(2,1)} %constant.8.clone.time_hbm, bf16[1024,1024]{1,0:T(8,128)(2,1)} %constant.11.clone.channel_hbm, bf16[16,512]{1,0:T(8,128)(2,1)} %filter_taps.1, s32[32,128]{1,0:T(8,128)} %bitcast.4, s32[1,256]{1,0:T(1,128)} %bitcast.5, ...), custom_call_target="tpu_custom_call" | custom-call | tf_op jit(solution)/shard_map/pallas_call | solution.py:356
  34.7 1.4 %copy.10 = f32[1,32,256]{2,1,0:T(8,128)} copy(f32[1,32,256]{2,1,0:T(8,128)} %bitcast.3) | data formatting | bytes 65536
